TPU v7x, 32 devices: a whole 2x2x4 slice. The times are simulated.
32 devices in a mesh: parts: 2 (over y), group: 4 (over z), tensor: 4 (over x, core).
Axes of the slice: x: 2, y: 2, z: 4, core: 2. Of those that a mesh axis runs over, the one named last changes fastest.
Arguments:
- queries: bfloat16 [512, 8192], P(('parts', 'group'), 'tensor'), parts along dimension 0, may hold values from -36 to 36
- keys: bfloat16 [512, 1024], P(('parts', 'group'), 'tensor'), parts along dimension 0, may hold values from -64 to 64
- values: bfloat16 [512, 1024], P(('parts', 'group'), 'tensor'), parts along dimension 0, may hold values from -6 to 6
- prefix_keys: bfloat16 [2048, 1024], P(('parts', 'group'), 'tensor'), parts along dimension 0, may hold values from -6 to 6
- prefix_values: bfloat16 [2048, 1024], P(('parts', 'group'), 'tensor'), parts along dimension 0, may hold values from -6 to 6
- spread: int32 [8], P('parts'), parts along dimension 0, may hold values from 0 to 3, as said below
- turn: int32 [8], P('parts'), parts along dimension 0, may hold values from 0 to 7
- new_blocks: int32 [8, 4], P('parts'), parts along dimension 0, may hold values from 1 to 2, as said below
- prefix_len: int32 [8, 4], P('parts'), parts along dimension 0, may hold values from 1 to 64, as said below
- owner: int32 [8, 4], P('parts'), parts along dimension 0, may hold values from 0 to 3, as said below
- page_start: int32 [8, 4], P('parts'), parts along dimension 0, may hold values from 0 to 6, as said below
Outputs:
- attention: bfloat16 [512, 8192], P(('parts', 'group'), 'tensor'), parts along dimension 0
- cache: bfloat16 [64, 2, 8, 1024], P(('parts', 'group'), None, 'tensor'), parts along dimension 0
There are 2 independent parts, one for each index of `parts`. A program takes and returns all parts, laid end to end along the dimension named above; each array names one. Nothing has to cross between parts.
Inputs may be any that keep to these rules, and one draw needn't show every extreme that they name: `spread`: A permutation of the numbers below 4. `new_blocks`: in every group one prompt has exactly 2 new blocks. `prefix_len`: in every group one prompt has exactly 64 cached tokens. `owner`: the prompts of one prefill group have different owners, and every decode group owns exactly one prompt of each index p. `page_start`: A multiple of 2; the prompts owned by one decode group start at different pages.
All inputs are finite; a program needn't handle non-finite values.
Results may differ from a plain program's by a relative error of at most 0.012.
The roundings to bfloat16 on the way count: a program that leaves them out, or rounds other values in their place, can miss the bound.
Values may be sent and summed in bfloat16 or wider, within the bound.
No kernel may reach another device: no remote copies, remote signals or barrier semaphores. Data moves between devices by JAX's collectives and lax.ppermute only.
A program may use at most 64 MiB of HBM per device.

v0:
```python
import math

import jax
import jax.numpy as jnp
from jax import lax
from jax.sharding import PartitionSpec as P

HEAD = 128
BLOCK = 8
MAXP = 2
CTXP = 64


def rotate(tensor_in, position):
    half_width = tensor_in.shape[-1] // 2
    ladder = jnp.arange(half_width, dtype=jnp.int32).astype(jnp.float32)
    frequency = jnp.exp(ladder * (-2.0 * math.log(500000.0) / tensor_in.shape[-1]))
    angles = position.astype(jnp.float32)[:, None] * frequency[None, :]
    cosine = jnp.cos(angles)[:, None, :]
    sine_part = jnp.sin(angles)[:, None, :]
    first_half = tensor_in[..., :half_width].astype(jnp.float32)
    second = tensor_in[..., half_width:].astype(jnp.float32)
    joined = jnp.concatenate(
        [first_half * cosine - second * sine_part, second * cosine + first_half * sine_part],
        axis=-1,
    )
    return joined.astype(jnp.bfloat16)


def layout(lengths, prefix, slot_count, block_rows):
    prompt_ends = jnp.cumsum(lengths)
    starts = prompt_ends - lengths
    slot_index = jnp.arange(slot_count, dtype=jnp.int32)
    segment = jnp.sum((slot_index[:, None] >= prompt_ends[None, :]).astype(jnp.int32), axis=1)
    prompt_index = jnp.arange(lengths.shape[0], dtype=jnp.int32)
    member = (segment[:, None] == prompt_index[None, :]).astype(jnp.int32)
    first_slot = jnp.sum(member * starts[None, :], axis=1)
    offset = jnp.sum(member * prefix[None, :], axis=1)
    token_index = jnp.arange(block_rows, dtype=jnp.int32)
    position = (offset + (slot_index - first_slot) * block_rows)[:, None] + token_index[None, :]
    return (segment, starts, position.reshape(-1))


def allowed(row_segment, prefix, context):
    prompt_count = prefix.shape[0]
    region = jnp.arange(prompt_count * context, dtype=jnp.int32)
    region_prompt = region // context
    prompt_index = jnp.arange(prompt_count, dtype=jnp.int32)
    region_limit = jnp.sum(
        jnp.where(region_prompt[:, None] == prompt_index[None, :], prefix[None, :], 0), axis=1
    )
    cached = (row_segment[:, None] == region_prompt[None, :]) & (region % context < region_limit)[
        None, :
    ]
    row_index = jnp.arange(row_segment.shape[0], dtype=jnp.int32)
    fresh_keys = (row_segment[:, None] == row_segment[None, :]) & (
        row_index[None, :] <= row_index[:, None]
    )
    return jnp.concatenate([cached, fresh_keys], axis=1)


def normalize(scores, key_mask):
    masked = jnp.where(key_mask, scores, -1e30)
    row_top = jnp.max(masked, axis=-1, keepdims=True)
    row_exps = jnp.exp(masked - row_top)
    return (row_exps / jnp.sum(row_exps, axis=-1, keepdims=True)).astype(jnp.bfloat16)


def per_device(
    queries,
    keys,
    values,
    prefix_keys,
    prefix_values,
    spread,
    turn,
    new_blocks,
    prefix_len,
    owner,
    page_start,
):
    groups = lax.axis_size("group")
    own_group = lax.axis_index("group")
    width_q = queries.shape[1]
    width_k = keys.shape[1]
    heads_q = width_q // HEAD
    heads_k = width_k // HEAD
    head_ratio = heads_q // heads_k
    slot_count = queries.shape[0] // BLOCK
    slot_rows = slot_count * BLOCK
    prompt_count = new_blocks.shape[1]
    capacity = (slot_count + groups - 1) // groups
    score_scale = 1.0 / math.sqrt(HEAD)
    group_index = jnp.arange(groups, dtype=jnp.int32)
    slot_index = jnp.arange(slot_count, dtype=jnp.int32)
    inverse = jnp.sum(
        jnp.where(spread[None, :] == group_index[:, None], group_index[None, :], 0), axis=1
    )
    distance = (own_group - group_index) % groups
    sent_slot = inverse[distance][:, None] + groups * jnp.arange(capacity, dtype=jnp.int32)[None, :]
    source_slot = (sent_slot + turn[own_group]) % slot_count

    def outgoing(source_rows):
        return jnp.take(
            source_rows.reshape(slot_count, BLOCK, source_rows.shape[1]), source_slot, axis=0
        )

    arrived = (
        lax.all_to_all(outgoing(queries), "group", split_axis=0, concat_axis=0, tiled=True),
        lax.all_to_all(outgoing(keys), "group", split_axis=0, concat_axis=0, tiled=True),
        lax.all_to_all(outgoing(values), "group", split_axis=0, concat_axis=0, tiled=True),
    )
    root = (own_group + spread[slot_index % groups]) % groups
    flat_index = root * capacity + slot_index // groups

    def placed(received):
        gathered = jnp.take(
            received.reshape(groups * capacity, BLOCK, received.shape[3]), flat_index, axis=0
        )
        return gathered.reshape(slot_rows, received.shape[3])

    packed_q = placed(arrived[0])
    packed_k = placed(arrived[1])
    packed_v = placed(arrived[2])
    lengths = new_blocks[own_group]
    prefix = prefix_len[own_group]
    segment, starts, position = layout(lengths, prefix, slot_count, BLOCK)
    rot_q = rotate(packed_q.reshape(slot_rows, heads_q, HEAD), position)
    rot_k = rotate(packed_k.reshape(slot_rows, heads_k, HEAD), position)
    row_segment = jnp.repeat(segment, BLOCK)
    kv_order = jnp.arange(heads_q, dtype=jnp.int32) // head_ratio
    key_stack = jnp.concatenate([prefix_keys, rot_k.reshape(slot_rows, width_k)], axis=0).reshape(
        -1, heads_k, HEAD
    )
    value_stack = jnp.concatenate([prefix_values, packed_v], axis=0).reshape(-1, heads_k, HEAD)
    key_mask = allowed(row_segment, prefix, CTXP)

    def head_scores(operands):
        query_head, kv_index = operands
        key_head = lax.dynamic_index_in_dim(key_stack, kv_index, axis=1, keepdims=False)
        value_head = lax.dynamic_index_in_dim(value_stack, kv_index, axis=1, keepdims=False)
        scores = (
            lax.dot_general(
                query_head, key_head, (((1,), (1,)), ((), ())), preferred_element_type=jnp.float32
            )
            * score_scale
        )
        weights = normalize(scores, key_mask)
        return jnp.dot(weights, value_head, preferred_element_type=jnp.float32)

    heads_out = lax.map(head_scores, (jnp.transpose(rot_q, (1, 0, 2)), kv_order))
    mixed = jnp.transpose(heads_out, (1, 0, 2)).reshape(slot_rows, width_q)
    attention = jnp.where((row_segment < prompt_count)[:, None], mixed, 0.0).astype(jnp.bfloat16)
    kv_blocks = jnp.stack(
        [rot_k.reshape(slot_count, BLOCK, width_k), packed_v.reshape(slot_count, BLOCK, width_k)],
        axis=1,
    )
    routed = owner[own_group][None, :] == group_index[:, None]
    has_prompt = jnp.any(routed, axis=1)
    first_slot = jnp.sum(jnp.where(routed, starts[None, :], 0), axis=1)
    block_total = jnp.sum(jnp.where(routed, lengths[None, :], 0), axis=1)
    step_index = jnp.arange(MAXP, dtype=jnp.int32)
    slot_pick = jnp.clip(first_slot[:, None] + step_index[None, :], 0, slot_count - 1)
    keep_slot = has_prompt[:, None] & (step_index[None, :] < block_total[:, None])
    chosen = jnp.take(kv_blocks, slot_pick, axis=0)
    received = lax.all_to_all(
        lax.all_to_all(
            jnp.where(keep_slot[:, :, None, None, None], chosen, jnp.zeros_like(chosen)),
            "group",
            split_axis=0,
            concat_axis=0,
            tiled=True,
        ),
        "tensor",
        split_axis=3,
        concat_axis=4,
        tiled=True,
    )
    owned_here = owner == own_group
    sender = jnp.sum(jnp.where(owned_here, group_index[:, None], 0), axis=0)
    region = jnp.sum(jnp.where(owned_here, page_start, 0), axis=0) // MAXP
    page_count = prompt_count * MAXP
    page_index = jnp.arange(page_count, dtype=jnp.int32)
    page_match = (page_index // MAXP)[:, None] == region[None, :]
    from_sender = jnp.sum(jnp.where(page_match, sender[None, :], 0), axis=1)
    gather_at = from_sender * MAXP + page_index % MAXP
    cache = jnp.take(
        received.reshape(groups * MAXP, 2, received.shape[3], received.shape[4]), gather_at, axis=0
    )
    return (attention, cache)


def solution(mesh):
    return jax.shard_map(
        per_device,
        mesh=mesh,
        in_specs=(
            P(("parts", "group"), "tensor"),
            P(("parts", "group"), "tensor"),
            P(("parts", "group"), "tensor"),
            P(("parts", "group"), "tensor"),
            P(("parts", "group"), "tensor"),
            P("parts"),
            P("parts"),
            P("parts", None),
            P("parts", None),
            P("parts", None),
            P("parts", None),
        ),
        out_specs=(P(("parts", "group"), "tensor"), P(("parts", "group"), None, "tensor", None)),
        check_vma=False,
    )
```

profile of v0, /device:TPU:0, one launch (start us, length us, event | category | flops | bytes accessed | tf_op | source)
XLA Modules:
  0.0 116.9 jit_solution(9049304483131018788)
XLA Ops:
  0.7 0.7 copy-done.1
  3.4 0.7 compare_and_fusion.3
  4.1 0.7 compare_select_fusion.3
  6.2 0.7 broadcast_select_fusion.6
  6.9 6.3 %all-to-all-start.2 = ((bf16[4,2,8,256]{3,2,1,0:T(8,128)(2,1)}), bf16[4,2,8,256]{3,2,1,0:T(8,128)(2,1)S(1)}, u32[]{:S(2)}, u32[]{:S(2)}) async-start(bf16[4,2,8,256]{3,2,1,0:T(8,128)(2,1)} %get-tuple-element.113), calls=%async_computation.2 | async-start | bytes 65536 | tf_op jit(solution)/shard_map/all_to_all | solution.py:111
  14.1 0.7 copy-done.8
  15.0 0.7 fusion.30
  16.8 0.7 compare_select_fusion.2
  19.0 0.8 broadcast_select_fusion
  20.2 5.1 %all-to-all-start.1 = ((bf16[4,2,8,256]{3,2,1,0:T(8,128)(2,1)}), bf16[4,2,8,256]{3,2,1,0:T(8,128)(2,1)S(1)}, u32[]{:S(2)}, u32[]{:S(2)}) async-start(bf16[4,2,8,256]{3,2,1,0:T(8,128)(2,1)} %get-tuple-element.114), calls=%async_computation.1 | async-start | bytes 65536 | tf_op jit(solution)/shard_map/all_to_all | solution.py:110
  26.0 4.9 %all-to-all-done.1 = bf16[4,2,8,256]{3,2,1,0:T(8,128)(2,1)S(1)} async-done(((bf16[4,2,8,256]{3,2,1,0:T(8,128)(2,1)}), bf16[4,2,8,256]{3,2,1,0:T(8,128)(2,1)S(1)}, u32[]{:S(2)}, u32[]{:S(2)}) %all-to-all-start.1) | async-done | bytes 32800 | tf_op jit(solution)/shard_map/all_to_all | solution.py:110
  32.7 0.8 broadcast_select_fusion.3
  33.4 3.3 %all-to-all-start.3 = ((bf16[4,2,2,8,256]{4,2,1,3,0:T(2,128)(2,1)}), bf16[4,2,2,8,256]{4,2,1,3,0:T(2,128)(2,1)S(1)}, u32[]{:S(2)}, u32[]{:S(2)}) async-start(bf16[4,2,2,8,256]{4,2,1,3,0:T(2,128)(2,1)} %broadcast_select_fusion.3), calls=%async_computation.3 | async-start | bytes 131072 | tf_op jit(solution)/shard_map/all_to_all | solution.py:167
  36.8 5.7 %all-to-all-done.3 = bf16[4,2,2,8,256]{4,2,1,3,0:T(2,128)(2,1)S(1)} async-done(((bf16[4,2,2,8,256]{4,2,1,3,0:T(2,128)(2,1)}), bf16[4,2,2,8,256]{4,2,1,3,0:T(2,128)(2,1)S(1)}, u32[]{:S(2)}, u32[]{:S(2)}) %all-to-all-start.3) | async-done | bytes 65568 | tf_op jit(solution)/shard_map/all_to_all | solution.py:167
  42.4 0.7 copy.74
  43.1 3.3 %all-to-all-start.4 = ((bf16[4,2,2,8,256]{4,2,1,0,3:T(2,128)(2,1)}), bf16[4,2,2,8,256]{4,2,1,0,3:T(2,128)(2,1)S(1)}, u32[]{:S(2)}, u32[]{:S(2)}) async-start(bf16[4,2,2,8,256]{4,2,1,0,3:T(2,128)(2,1)} %copy.74), calls=%async_computation.4 | async-start | bytes 131072 | tf_op jit(solution)/shard_map/all_to_all | solution.py:166
  46.7 0.8 copy-done.3
  47.6 2.9 %all-to-all-done.4 = bf16[4,2,2,8,256]{4,2,1,0,3:T(2,128)(2,1)S(1)} async-done(((bf16[4,2,2,8,256]{4,2,1,0,3:T(2,128)(2,1)}), bf16[4,2,2,8,256]{4,2,1,0,3:T(2,128)(2,1)S(1)}, u32[]{:S(2)}, u32[]{:S(2)}) %all-to-all-start.4) | async-done | bytes 65568 | tf_op jit(solution)/shard_map/all_to_all | solution.py:166
  50.5 3.4 %all-to-all-start = ((bf16[4,2,8,2048]{3,2,1,0:T(8,128)(2,1)}), bf16[4,2,8,2048]{3,2,1,0:T(8,128)(2,1)S(1)}, u32[]{:S(2)}, u32[]{:S(2)}) async-start(bf16[4,2,8,2048]{3,2,1,0:T(8,128)(2,1)} %broadcast_select_fusion), calls=%async_computation | async-start | bytes 524288 | tf_op jit(solution)/shard_map/all_to_all | solution.py:109
  54.6 0.7 gather_fusion.5
  55.3 0.8 broadcast_select_fusion.1
  56.0 6.9 %all-to-all-done = bf16[4,2,8,2048]{3,2,1,0:T(8,128)(2,1)S(1)} async-done(((bf16[4,2,8,2048]{3,2,1,0:T(8,128)(2,1)}), bf16[4,2,8,2048]{3,2,1,0:T(8,128)(2,1)S(1)}, u32[]{:S(2)}, u32[]{:S(2)}) %all-to-all-start) | async-done | bytes 262176 | tf_op jit(solution)/shard_map/all_to_all | solution.py:109
  64.1 51.9 %while.10 = (s32[]{:T(128)}, bf16[16,64,128]{2,1,0:T(8,128)(2,1)S(1)}, bf16[16,64,128]{2,1,0:T(8,128)(2,1)S(1)}, s32[16]{0:T(128)S(1)}, bf16[320,2,128]{2,0,1:T(...) while((s32[]{:T(128)}, ...), condition=%wide.region_9.12_spmd, body=%wide.region_6.11_spmd.sunk | while | flops 10649477 | bytes 501675 | solution.py:151
  116.1 0.8 fusion.17
  (170 shorter events, 32.4 us)
Async XLA Ops:
  0.6 17.8 %copy-start = (bf16[64,2048]{1,0:T(8,128)(2,1)S(1)}, bf16[64,2048]{1,0:T(8,128)(2,1)}, u32[]{:S(2)}) copy-start(bf16[64,2048]{1,0:T(8,128)(2,1)} %param.17) | copy-start | bytes 786436
  0.7 0.7 copy-start.1
  1.5 0.7 copy-start.9
  2.7 2.2 %copy-start.4 = (bf16[64,256]{1,0:T(8,128)(2,1)S(1)}, bf16[64,256]{1,0:T(8,128)(2,1)}, u32[]{:S(2)}) copy-start(bf16[64,256]{1,0:T(8,128)(2,1)} %param.19) | copy-start | bytes 98308
  4.9 0.8 copy-start.5
  6.9 13.2 %all-to-all-start.2 = ((bf16[4,2,8,256]{3,2,1,0:T(8,128)(2,1)}), bf16[4,2,8,256]{3,2,1,0:T(8,128)(2,1)S(1)}, u32[]{:S(2)}, u32[]{:S(2)}) async-start(bf16[4,2,8,256]{3,2,1,0:T(8,128)(2,1)} %get-tuple-element.113), calls=%async_computation.2 | async-start | bytes 65536 | tf_op jit(solution)/shard_map/all_to_all | solution.py:111
  13.3 0.7 copy-start.7
  13.3 0.7 copy-start.6
  14.1 0.7 copy-start.8
  20.2 10.8 %all-to-all-start.1 = ((bf16[4,2,8,256]{3,2,1,0:T(8,128)(2,1)}), bf16[4,2,8,256]{3,2,1,0:T(8,128)(2,1)S(1)}, u32[]{:S(2)}, u32[]{:S(2)}) async-start(bf16[4,2,8,256]{3,2,1,0:T(8,128)(2,1)} %get-tuple-element.114), calls=%async_computation.1 | async-start | bytes 65536 | tf_op jit(solution)/shard_map/all_to_all | solution.py:110
  33.4 9.0 %all-to-all-start.3 = ((bf16[4,2,2,8,256]{4,2,1,3,0:T(2,128)(2,1)}), bf16[4,2,2,8,256]{4,2,1,3,0:T(2,128)(2,1)S(1)}, u32[]{:S(2)}, u32[]{:S(2)}) async-start(bf16[4,2,2,8,256]{4,2,1,3,0:T(2,128)(2,1)} %broadcast_select_fusion.3), calls=%async_computation.3 | async-start | bytes 131072 | tf_op jit(solution)/shard_map/all_to_all | solution.py:167
  36.7 9.9 %copy-start.2 = (bf16[256,256]{1,0:T(8,128)(2,1)S(1)}, bf16[256,256]{1,0:T(8,128)(2,1)}, u32[]{:S(2)}) copy-start(bf16[256,256]{1,0:T(8,128)(2,1)} %param.20) | copy-start | bytes 393220
  43.1 7.4 %all-to-all-start.4 = ((bf16[4,2,2,8,256]{4,2,1,0,3:T(2,128)(2,1)}), bf16[4,2,2,8,256]{4,2,1,0,3:T(2,128)(2,1)S(1)}, u32[]{:S(2)}, u32[]{:S(2)}) async-start(bf16[4,2,2,8,256]{4,2,1,0,3:T(2,128)(2,1)} %copy.74), calls=%async_computation.4 | async-start | bytes 131072 | tf_op jit(solution)/shard_map/all_to_all | solution.py:166
  46.6 0.9 copy-start.3
  50.5 12.4 %all-to-all-start = ((bf16[4,2,8,2048]{3,2,1,0:T(8,128)(2,1)}), bf16[4,2,8,2048]{3,2,1,0:T(8,128)(2,1)S(1)}, u32[]{:S(2)}, u32[]{:S(2)}) async-start(bf16[4,2,8,2048]{3,2,1,0:T(8,128)(2,1)} %broadcast_select_fusion), calls=%async_computation | async-start | bytes 524288 | tf_op jit(solution)/shard_map/all_to_all | solution.py:109
where the time goes:
time: 118 us; the launch traced here: 117 us
  loops' own time  31.5 us (27%)
  local copies, waits for them, and re-layouts  23 us (19%)
  starting transfers between devices  21.4 us (18%)
  waiting for transfers between devices  20.4 us (17%)
  other arithmetic  11.6 us (10%)
  matrix products  7.96 us (7%)
    another operation x1, loops' own time, per_device(): lax.map(head_scores, (jnp.transpose(rot_q, (1, 0, 2)), kv_order))  31.5 us
    dynamic_slice x16, local copies, waits for them, and re-layouts, per_device(): lax.map(head_scores, (jnp.transpose(rot_q, (1, 0, 2)), kv_order))  9.38 us
    all_to_all x1, waiting for transfers between devices, per_device(): lax.all_to_all(outgoing(queries), 'group', split_axis=0, concat_axis=0, t...  6.87 us
    all_to_all x1, starting transfers between devices, per_device(): lax.all_to_all(outgoing(values), 'group', split_axis=0, concat_axis=0, ti...  6.32 us
    all_to_all x1, waiting for transfers between devices, per_device(): lax.all_to_all(jnp.where(keep_slot[:, :, None, None, None], chosen, jnp.z...  5.68 us
    all_to_all x1, starting transfers between devices, per_device(): lax.all_to_all(outgoing(keys), 'group', split_axis=0, concat_axis=0, tile...  5.1 us
    all_to_all x1, waiting for transfers between devices, per_device(): lax.all_to_all(outgoing(keys), 'group', split_axis=0, concat_axis=0, tile...  4.92 us
    dot_general x16, matrix products, head_scores(): lax.dot_general(query_head, key_head, (((1,), (1,)), ((), ())), preferred...  4.28 us
  transfers between devices with their start and end apart: 5, of which 4 were waited for; matrix products, arithmetic and copies ran while one was open for 7% of the time, Pallas kernels for 0%

commit v1 on v0

v1 whole, which is shorter than its diff:
```python
import functools
import math

import jax
import jax.numpy as jnp
import numpy as np
from jax import lax
from jax.experimental import pallas as pl
from jax.experimental.pallas import tpu as pltpu
from jax.sharding import PartitionSpec as P

HEAD = 128
BLOCK = 8
MAXP = 2
CTXP = 64
VMEM_LIMIT = 48 * 1024 * 1024

SMEM = pl.BlockSpec(memory_space=pltpu.SMEM)
VMEM = pl.BlockSpec(memory_space=pltpu.VMEM)
ANY = pl.BlockSpec(memory_space=pl.ANY)


def rope_table():
    count = CTXP + MAXP * BLOCK
    half = HEAD // 2
    frequency = np.exp(np.arange(half) * (-2.0 * math.log(500000.0) / HEAD))
    angles = np.arange(count)[:, None] * frequency[None, :]
    cosine, sine = np.cos(angles), np.sin(angles)
    return (
        np.concatenate([cosine, cosine], axis=1).astype(np.float32),
        np.concatenate([-sine, sine], axis=1).astype(np.float32),
    )


def loop(count, body, unrolled=16):
    if count <= unrolled:
        for index in range(count):
            body(index)
    else:
        lax.fori_loop(0, count, lambda index, carry: (body(index), carry)[1], 0)


def turned(head_block, cosine, sine):
    return head_block * cosine + pltpu.roll(head_block, HEAD // 2, 1) * sine


def dispatch_kernel(groups, spread, turn, queries, keys, values, out, sem):
    own = lax.axis_index("group")
    slots, _, width_q = queries.shape
    width_k = keys.shape[2]
    capacity = slots // groups

    def column(c):
        target = lax.rem(own - spread[c] + groups, groups)
        for step in range(capacity):
            source = lax.rem(c + groups * step + turn[own], slots)
            at = out.at[target, step]
            for ref, first, width in (
                (queries, 0, width_q),
                (keys, width_q, width_k),
                (values, width_q + width_k, width_k),
            ):
                pltpu.make_async_copy(ref.at[source], at.at[:, pl.ds(first, width)], sem).start()

    loop(groups, column)
    pltpu.make_async_copy(out, out, sem).wait()


def slot_table(own, new_blocks, prefix_len, prompt, offset, live):
    prompts = new_blocks.shape[1]
    slots = live.shape[0]

    def clear(j):
        prompt[j] = 0
        offset[j] = 0
        live[j] = 0

    loop(slots, clear)

    def one(p, start):
        blocks = new_blocks[own, p]
        cached = prefix_len[own, p]
        for step in range(MAXP):
            at = jnp.minimum(start + step, slots - 1)

            @pl.when(step < blocks)
            def _():
                prompt[at] = p
                offset[at] = cached + step * BLOCK
                live[at] = 1 + step

        return start + blocks

    lax.fori_loop(0, prompts, one, 0)


def pages_kernel(
    groups, tensors, spread, turn, new_blocks, prefix_len, owner, keys, values, cosine, sine, out, rows,
    dest_group, dest_owner,
):
    own = lax.axis_index("group")
    slots, _, width_k = keys.shape
    capacity = slots // groups
    prompts = new_blocks.shape[1]
    tokens = BLOCK // tensors

    def column(c):
        target = lax.rem(own - spread[c] + groups, groups)
        for step in range(capacity):
            j = c + groups * step
            source = lax.rem(j + turn[own], slots)

            def find(p, carry):
                start, place, holder = carry
                blocks = new_blocks[target, p]
                inside = (j >= start) & (j < start + blocks)
                place = jnp.where(inside, prefix_len[target, p] + (j - start) * BLOCK, place)
                holder = jnp.where(inside, owner[target, p], holder)
                return start + blocks, place, holder

            carry = (jnp.int32(0), jnp.int32(0), jnp.int32(-1))
            if prompts <= 8:
                for p in range(prompts):
                    carry = find(p, carry)
            else:
                carry = lax.fori_loop(0, prompts, find, carry)
            _, place, holder = carry
            dest_group[source] = target
            dest_owner[source] = holder
            cos = cosine[pl.ds(place, BLOCK), :]
            sin = sine[pl.ds(place, BLOCK), :]
            block = keys[source].astype(jnp.float32)
            at = pl.multiple_of(source * BLOCK, BLOCK)
            rows[pl.ds(at, BLOCK), :] = jnp.concatenate(
                [
                    turned(block[:, h * HEAD : (h + 1) * HEAD], cos, sin)
                    for h in range(width_k // HEAD)
                ],
                axis=1,
            )
            at = pl.multiple_of((slots + source) * BLOCK, BLOCK)
            rows[pl.ds(at, BLOCK), :] = values[source].astype(jnp.float32)

    loop(groups, column)
    body = rows[...].astype(jnp.bfloat16)
    part = 2 * tokens
    shape = (tensors * groups * part, 2 * slots * BLOCK)
    row = lax.broadcasted_iota(jnp.int32, shape, 0)
    col = lax.broadcasted_iota(jnp.int32, shape, 1)
    row_tensor = row // (groups * part)
    row_group = (row // part) % groups
    same = ((row // tokens) % 2 == col // (slots * BLOCK)) & (
        row_tensor * tokens + row % tokens == col % BLOCK
    )
    code = jnp.where(same, row_group * slots + (col // BLOCK) % slots, -1)

    def send(d):
        def mark(b, total):
            wanted = jnp.where(dest_owner[b] == d, dest_group[b] * slots + b, -2)
            return total | (code == wanted)

        if slots <= 8:
            total = code == -2
            for b in range(slots):
                total = mark(b, total)
            pick = total.astype(jnp.float32)
        else:
            pick = lax.fori_loop(
                0,
                slots,
                lambda b, total: jnp.where(
                    code == jnp.where(dest_owner[b] == d, dest_group[b] * slots + b, -2), 1.0, total
                ),
                jnp.zeros(shape, jnp.float32),
            )
        moved = jnp.dot(pick.astype(jnp.bfloat16), body, preferred_element_type=jnp.float32)
        out[pl.ds(d * tensors, tensors)] = moved.astype(jnp.bfloat16).reshape(
            tensors, groups * part, width_k
        )

    loop(groups, send)


def attention_kernel(
    groups, heads_q, heads_k, spread, new_blocks, prefix_len, arrived, prefix_keys, prefix_values, cosine, sine,
    out, prompt, offset, live,
):
    own = lax.axis_index("group")
    slots = out.shape[0]
    ratio = heads_q // heads_k
    width_q = heads_q * HEAD
    width_k = heads_k * HEAD
    slot_table(own, new_blocks, prefix_len, prompt, offset, live)
    scale = math.log2(math.e) / math.sqrt(HEAD)
    span = CTXP + 2 * BLOCK
    rows = ratio * BLOCK
    lane = lax.broadcasted_iota(jnp.int32, (rows, span), 1)
    token = lax.broadcasted_iota(jnp.int32, (rows, span), 0) % BLOCK
    fresh = (lane >= CTXP + BLOCK) & (lane - (CTXP + BLOCK) <= token)
    before = (lane >= CTXP) & (lane < CTXP + BLOCK)

    def slot(j):
        p, place, state = prompt[j], offset[j], live[j]
        root = lax.rem(own + spread[lax.rem(j, groups)], groups)
        jj = jnp.maximum(j - 1, 0)
        back = lax.rem(own + spread[lax.rem(jj, groups)], groups)
        here = arrived.at[root, j // groups]
        prev = arrived.at[back, jj // groups]
        cos = cosine[pl.ds(place, BLOCK), :]
        sin = sine[pl.ds(place, BLOCK), :]
        early = jnp.maximum(place - BLOCK, 0)
        cos_prev = cosine[pl.ds(early, BLOCK), :]
        sin_prev = sine[pl.ds(early, BLOCK), :]
        region = pl.ds(pl.multiple_of(p * CTXP, CTXP), CTXP)
        cached = prefix_len[own, p]
        mask = fresh | (lane < jnp.minimum(cached, CTXP)) | (before & (state == 2))
        for h in range(heads_k):
            at = slice(width_q + h * HEAD, width_q + (h + 1) * HEAD)
            new_key = jnp.concatenate(
                [
                    turned(prev[:, at].astype(jnp.float32), cos_prev, sin_prev),
                    turned(here[:, at].astype(jnp.float32), cos, sin),
                ],
                axis=0,
            ).astype(jnp.bfloat16)
            at = slice(width_q + width_k + h * HEAD, width_q + width_k + (h + 1) * HEAD)
            new_value = jnp.concatenate(
                [prev[:, at].astype(jnp.float32), here[:, at].astype(jnp.float32)], axis=0
            ).astype(jnp.bfloat16)
            at = slice(h * HEAD, (h + 1) * HEAD)
            key = jnp.concatenate([prefix_keys[region, at], new_key], axis=0)
            value = jnp.concatenate([prefix_values[region, at], new_value], axis=0)
            query = jnp.concatenate(
                [
                    turned(here[:, n * HEAD : (n + 1) * HEAD].astype(jnp.float32), cos, sin)
                    for n in range(h * ratio, (h + 1) * ratio)
                ],
                axis=0,
            ).astype(jnp.bfloat16)
            scores = lax.dot_general(
                query, key, (((1,), (1,)), ((), ())), preferred_element_type=jnp.float32
            )
            scores = jnp.where(mask, scores, -1e30)
            top = jnp.max(scores, axis=1, keepdims=True)
            powers = jnp.exp2((scores - top) * scale)
            weights = powers / jnp.sum(powers, axis=1, keepdims=True)
            mixed = jnp.dot(weights.astype(jnp.bfloat16), value, preferred_element_type=jnp.float32)
            mixed = jnp.where(state > 0, mixed, 0.0)
            for n in range(ratio):
                first = (h * ratio + n) * HEAD
                out[j, :, first : first + HEAD] = mixed[n * BLOCK : (n + 1) * BLOCK].astype(
                    jnp.bfloat16
                )

    loop(slots, slot)


def cache_kernel(groups, tensors, spread, new_blocks, owner, page_start, arrived, out, source):
    own = lax.axis_index("group")
    prompts = new_blocks.shape[1]
    tokens = BLOCK // tensors
    part = 2 * tokens
    pages = prompts * MAXP

    def of_group(g):
        def one(p, start):
            blocks = new_blocks[g, p]
            mine = owner[g, p] == own
            for step in range(MAXP):
                j = start + step
                root = lax.rem(g + spread[lax.rem(j, groups)], groups)
                at = jnp.where(mine, page_start[g, p] + step, pages)
                source[at] = jnp.where(step < blocks, root * groups + g, -1)
            return start + blocks

        start = jnp.int32(0)
        if prompts <= 8:
            for p in range(prompts):
                start = one(p, start)
        else:
            lax.fori_loop(0, prompts, one, start)

    loop(groups, of_group)
    shape = (pages * part, groups * groups * part)
    row = lax.broadcasted_iota(jnp.int32, shape, 0)
    col = lax.broadcasted_iota(jnp.int32, shape, 1)
    limit = groups * groups
    code = jnp.where(row % part == col % part, (row // part) * limit + col // part, -1)

    def mark(page, total):
        wanted = jnp.where(source[page] >= 0, page * limit + source[page], -2)
        return jnp.where(code == wanted, 1.0, total)

    pick = jnp.zeros(shape, jnp.float32)
    if pages <= 8:
        for page in range(pages):
            pick = mark(page, pick)
    else:
        pick = lax.fori_loop(0, pages, mark, pick)
    pick = pick.astype(jnp.bfloat16)
    width_k = arrived.shape[3]
    for t in range(tensors):
        body = arrived[:, t].reshape(groups * groups * part, width_k)
        moved = jnp.dot(pick, body, preferred_element_type=jnp.float32).astype(jnp.bfloat16)
        out[:, t * width_k : (t + 1) * width_k] = moved


def per_device(
    queries,
    keys,
    values,
    prefix_keys,
    prefix_values,
    spread,
    turn,
    new_blocks,
    prefix_len,
    owner,
    page_start,
):
    groups = lax.axis_size("group")
    tensors = lax.axis_size("tensor")
    width_q = queries.shape[1]
    width_k = keys.shape[1]
    heads_q = width_q // HEAD
    heads_k = width_k // HEAD
    slots = queries.shape[0] // BLOCK
    capacity = slots // groups
    prompts = new_blocks.shape[1]
    tokens = BLOCK // tensors
    pages = prompts * MAXP
    cosine, sine = (jnp.asarray(table) for table in rope_table())
    params = pltpu.CompilerParams(vmem_limit_bytes=VMEM_LIMIT)
    blocks_q = queries.reshape(slots, BLOCK, width_q)
    blocks_k = keys.reshape(slots, BLOCK, width_k)
    blocks_v = values.reshape(slots, BLOCK, width_k)

    sent = pl.pallas_call(
        functools.partial(dispatch_kernel, groups),
        out_shape=jax.ShapeDtypeStruct((groups, capacity, BLOCK, width_q + 2 * width_k), jnp.bfloat16),
        in_specs=[SMEM] * 2 + [ANY] * 3,
        out_specs=ANY,
        scratch_shapes=[pltpu.SemaphoreType.DMA],
        compiler_params=params,
        name="dispatch",
    )(spread, turn, blocks_q, blocks_k, blocks_v)
    arrived = lax.all_to_all(sent, "group", split_axis=0, concat_axis=0, tiled=True)

    finished = pl.pallas_call(
        functools.partial(pages_kernel, groups, tensors),
        out_shape=jax.ShapeDtypeStruct((groups * tensors, groups * 2 * tokens, width_k), jnp.bfloat16),
        in_specs=[SMEM] * 5 + [VMEM] * 4,
        out_specs=VMEM,
        scratch_shapes=[
            pltpu.VMEM((2 * slots * BLOCK, width_k), jnp.float32),
            pltpu.SMEM((slots,), jnp.int32),
            pltpu.SMEM((slots,), jnp.int32),
        ],
        compiler_params=params,
        name="finish_pages",
    )(spread, turn, new_blocks, prefix_len, owner, blocks_k, blocks_v, cosine, sine)
    handed = lax.all_to_all(finished, ("group", "tensor"), split_axis=0, concat_axis=0, tiled=True)

    attention = pl.pallas_call(
        functools.partial(attention_kernel, groups, heads_q, heads_k),
        out_shape=jax.ShapeDtypeStruct((slots, BLOCK, width_q), jnp.bfloat16),
        in_specs=[SMEM] * 3 + [VMEM] * 5,
        out_specs=VMEM,
        scratch_shapes=[pltpu.SMEM((slots,), jnp.int32)] * 3,
        compiler_params=params,
        name="attention",
    )(spread, new_blocks, prefix_len, arrived, prefix_keys, prefix_values, cosine, sine)

    cache = pl.pallas_call(
        functools.partial(cache_kernel, groups, tensors),
        out_shape=jax.ShapeDtypeStruct((pages * 2 * tokens, tensors * width_k), jnp.bfloat16),
        in_specs=[SMEM] * 4 + [VMEM],
        out_specs=VMEM,
        scratch_shapes=[pltpu.SMEM((pages + 1,), jnp.int32)],
        compiler_params=params,
        name="place_pages",
    )(
        spread,
        new_blocks,
        owner,
        page_start,
        handed.reshape(groups, tensors, groups * 2 * tokens, width_k),
    )
    return (
        attention.reshape(slots * BLOCK, width_q),
        cache.reshape(pages, 2, tokens, tensors * width_k),
    )


def solution(mesh):
    return jax.shard_map(
        per_device,
        mesh=mesh,
        in_specs=(
            P(("parts", "group"), "tensor"),
            P(("parts", "group"), "tensor"),
            P(("parts", "group"), "tensor"),
            P(("parts", "group"), "tensor"),
            P(("parts", "group"), "tensor"),
            P("parts"),
            P("parts"),
            P("parts", None),
            P("parts", None),
            P("parts", None),
            P("parts", None),
        ),
        out_specs=(P(("parts", "group"), "tensor"), P(("parts", "group"), None, "tensor", None)),
        check_vma=False,
    )
```

time: 118 us -> 44 us (0.37)
  loops' own time: 31.5 us -> 0 us
  local copies, waits for them, and re-layouts: 23 us -> 5.8 us
  other arithmetic: 11.6 us -> 0 us
  Pallas kernels: 0 us -> 10.7 us
  starting transfers between devices: 21.4 us -> 11.1 us
  matrix products: 7.96 us -> 0 us
  waiting for transfers between devices: 20.4 us -> 15 us
    another operation x1 -> x0, loops' own time: 31.5 us -> none  [per_device(): lax.map(head_scores, (jnp.transpose(rot_q, (1, 0, 2)), kv_order))]
    pallas_call x0 -> x4, Pallas kernels: none -> 10.7 us  [the longest x1 6.66 us: per_device(): pl.pallas_call(functools.partial(attention_kernel, groups, heads_q, heads...]
    all_to_all x5 -> x2, starting transfers between devices: 21.4 us -> 11.1 us  [the longest x1 7.49 us: per_device(): lax.all_to_all(finished, ('group', 'tensor'), split_axis=0, concat_axis=0...]
    dynamic_slice x17 -> x0, local copies, waits for them, and re-layouts: 9.96 us -> none  [the longest x16 9.38 us: per_device(): lax.map(head_scores, (jnp.transpose(rot_q, (1, 0, 2)), kv_order))]
    dot_general x32 -> x0, matrix products: 7.96 us -> none  [the longest x16 4.28 us: head_scores(): lax.dot_general(query_head, key_head, (((1,), (1,)), ((), ())), preferred...]
    gather x10 -> x0, local copies, waits for them, and re-layouts: 5.86 us -> none  [the longest x3 1.68 us: placed(): jnp.take(received.reshape(groups * capacity, BLOCK, received.shape[3]), f...]
    all_to_all x5 -> x2, waiting for transfers between devices: 20.4 us -> 15 us  [the longest x1 8.37 us: per_device(): lax.all_to_all(sent, 'group', split_axis=0, concat_axis=0, tiled=True)]
    select_n x17 -> x0, other arithmetic: 4.82 us -> none  [the longest x4 2.95 us: outgoing(): jnp.take(source_rows.reshape(slot_count, BLOCK, source_rows.shape[1]), so...]
  transfers between devices with their start and end apart: 5 -> 2, of which waited for: 4 -> 2; matrix products, arithmetic and copies ran while one was open for 7% -> 2% of each run, Pallas kernels for 0% -> 5%
where the time goes in v1:
time: 44 us; the launch traced here: 43.3 us
  waiting for transfers between devices  15 us (34%)
  starting transfers between devices  11.1 us (25%)
  Pallas kernels  10.7 us (24%)
  local copies, waits for them, and re-layouts  5.8 us (13%)
  between operations  0.79 us (2%)
    all_to_all x1, waiting for transfers between devices, per_device(): lax.all_to_all(sent, 'group', split_axis=0, concat_axis=0, tiled=True)  8.37 us
    all_to_all x1, starting transfers between devices, per_device(): lax.all_to_all(finished, ('group', 'tensor'), split_axis=0, concat_axis=0...  7.49 us
    pallas_call x1, Pallas kernels, per_device(): pl.pallas_call(functools.partial(attention_kernel, groups, heads_q, heads...  6.66 us
    all_to_all x1, waiting for transfers between devices, per_device(): lax.all_to_all(finished, ('group', 'tensor'), split_axis=0, concat_axis=0...  6.6 us
    unnamed x38, local copies, waits for them, and re-layouts  5.15 us
    all_to_all x1, starting transfers between devices, per_device(): lax.all_to_all(sent, 'group', split_axis=0, concat_axis=0, tiled=True)  3.58 us
    pallas_call x1, Pallas kernels, per_device(): pl.pallas_call(functools.partial(pages_kernel, groups, tensors), out_shap...  1.75 us
    pallas_call x1, Pallas kernels, per_device(): pl.pallas_call(functools.partial(dispatch_kernel, groups), out_shape=jax....  1.29 us
  transfers between devices with their start and end apart: 2, of which 2 were waited for; matrix products, arithmetic and copies ran while one was open for 2% of the time, Pallas kernels for 5%

profile of v1, /device:TPU:0, one launch (start us, length us, event | category | flops | bytes accessed | tf_op | source)
XLA Modules:
  0.0 43.3 jit_solution(18414991657979208367)
XLA Ops:
  0.6 0.0 copy-start.11
  0.6 0.0 copy-start.16
  0.7 0.0 copy-start.18
  0.7 0.7 %copy-done.11 = s32[4,4]{1,0:T(4,128)S(1)} copy-done((s32[4,4]{1,0:T(4,128)S(1)}, s32[4,4]{1,0:T(4,128)}, u32[]{:S(2)}) %copy-start.11) | copy-done | bytes 88
  1.3 0.0 copy-done.16
  1.3 0.8 %copy-done.1 = f32[80,128]{1,0:T(8,128)S(1)} copy-done((f32[80,128]{1,0:T(8,128)S(1)}, f32[80,128]{1,0:T(8,128)}, u32[]{:S(2)}) %copy-start.1) | copy-done | bytes 40984
  2.1 0.8 %copy-done.3 = f32[80,128]{1,0:T(8,128)S(1)} copy-done((f32[80,128]{1,0:T(8,128)S(1)}, f32[80,128]{1,0:T(8,128)}, u32[]{:S(2)}) %copy-start.3) | copy-done | bytes 40984
  2.9 0.8 %copy-done.7 = bf16[64,256]{1,0:T(8,128)(2,1)S(1)} copy-done((bf16[64,256]{1,0:T(8,128)(2,1)S(1)}, bf16[64,256]{1,0:T(8,128)(2,1)}, u32[]{:S(2)}) %copy-start.7) | copy-done | bytes 32792
  3.6 0.8 %copy-done.9 = bf16[64,256]{1,0:T(8,128)(2,1)S(1)} copy-done((bf16[64,256]{1,0:T(8,128)(2,1)S(1)}, bf16[64,256]{1,0:T(8,128)(2,1)}, u32[]{:S(2)}) %copy-start.9) | copy-done | bytes 32792
  4.4 0.7 %copy-done.12 = s32[4,4]{1,0:T(4,128)S(1)} copy-done((s32[4,4]{1,0:T(4,128)S(1)}, s32[4,4]{1,0:T(4,128)}, u32[]{:S(2)}) %copy-start.12) | copy-done | bytes 88
  5.1 0.7 %copy-done.14 = s32[4,4]{1,0:T(4,128)S(1)} copy-done((s32[4,4]{1,0:T(4,128)S(1)}, s32[4,4]{1,0:T(4,128)}, u32[]{:S(2)}) %copy-start.14) | copy-done | bytes 88
  5.8 1.8 %finish_pages.1 = bf16[16,16,256]{2,1,0:T(8,128)(2,1)} custom-call(s32[4]{0:T(128)S(1)} %copy-done.16, s32[4]{0:T(128)S(1)} %copy-done.18, s32[4,4]{1,0:T(4,128)S(1)} %copy-done.11, s32[4,4]{1,0:T(4,128)S(1)} %copy-done.14, s32[4,4]{1,0:T(4,128)S(1)} %copy-done.12, bf16[8,8,256]{2,1,0:T(8,128)(2,1)S(1)} %bitcast.7, bf16[8,8,256]{2,1,0:T(8,128)(2,1)S(1)} %bitcast.9, ...), custom_call_target="tpu_custom_call" | custom-call | tf_op jit(solution)/shard_map/finish_pages/pallas_call | solution.py:349
  7.5 7.5 %all-to-all-start.1 = ((bf16[16,16,256]{2,1,0:T(8,128)(2,1)}), bf16[16,16,256]{2,1,0:T(8,128)(2,1)S(1)}, u32[]{:S(2)}, u32[]{:S(2)}) async-start(bf16[16,16,256]{2,1,0:T(8,128)(2,1)} %finish_pages.1), calls=%async_computation.1 | async-start | bytes 262144 | tf_op jit(solution)/shard_map/all_to_all | solution.py:362
  15.0 1.3 %dispatch.1 = bf16[4,2,8,2560]{3,2,1,0:T(8,128)(2,1)} custom-call(s32[4]{0:T(128)S(1)} %copy-done.16, s32[4]{0:T(128)S(1)} %copy-done.18, bf16[8,8,2048]{2,1,0:T(8,128)(2,1)S(1)} %bitcast.6, bf16[8,8,256]{2,1,0:T(8,128)(2,1)S(1)} %bitcast.8, bf16[8,8,256]{2,1,0:T(8,128)(2,1)S(1)} %bitcast.10), custom_call_target="tpu_custom_call" | custom-call | tf_op jit(solution)/shard_map/dispatch/pallas_call | solution.py:338
  16.3 6.6 %all-to-all-done.1 = bf16[16,16,256]{2,1,0:T(8,128)(2,1)S(1)} async-done(((bf16[16,16,256]{2,1,0:T(8,128)(2,1)}), bf16[16,16,256]{2,1,0:T(8,128)(2,1)S(1)}, u32[]{:S(2)}, u32[]{:S(2)}) %all-to-all-start.1) | async-done | bytes 131104 | tf_op jit(solution)/shard_map/all_to_all | solution.py:362
  23.0 3.6 %all-to-all-start = ((bf16[4,2,8,2560]{3,2,1,0:T(8,128)(2,1)}), bf16[4,2,8,2560]{3,2,1,0:T(8,128)(2,1)S(1)}, u32[]{:S(2)}, u32[]{:S(2)}) async-start(bf16[4,2,8,2560]{3,2,1,0:T(8,128)(2,1)} %dispatch.1), calls=%async_computation | async-start | bytes 655360 | tf_op jit(solution)/shard_map/all_to_all | solution.py:347
  26.6 0.0 copy-start.5
  26.6 1.0 %place_pages.1 = bf16[32,1024]{1,0:T(8,128)(2,1)S(1)} custom-call(s32[4]{0:T(128)S(1)} %copy-done.16, s32[4,4]{1,0:T(4,128)S(1)} %copy-done.11, s32[4,4]{1,0:T(4,128)S(1)} %copy-done.13, s32[4,4]{1,0:T(4,128)S(1)} %copy-done.17, bf16[4,4,16,256]{3,2,1,0:T(8,128)(2,1)S(1)} %bitcast.5), custom_call_target="tpu_custom_call" | custom-call | tf_op jit(solution)/shard_map/place_pages/pallas_call | solution.py:374
  27.6 0.0 copy-start.2
  27.6 0.0 copy-start.4
  27.6 0.0 copy-start.15
  27.6 0.7 %reshape.27 = bf16[8,2,2,1024]{3,2,1,0:T(2,128)(2,1)} reshape(bf16[32,1024]{1,0:T(8,128)(2,1)S(1)} %place_pages.1) | data formatting | bytes 131072 | tf_op jit(solution)/shard_map/reshape | solution.py:391
  28.3 8.4 %all-to-all-done.arrived = bf16[4,2,8,2560]{3,2,1,0:T(8,128)(2,1)S(1)} async-done(((bf16[4,2,8,2560]{3,2,1,0:T(8,128)(2,1)}), bf16[4,2,8,2560]{3,2,1,0:T(8,128)(2,1)S(1)}, u32[]{:S(2)}, u32[]{:S(2)}) %all-to-all-start) | async-done | bytes 327712 | tf_op jit(solution)/shard_map/all_to_all | solution.py:347
  36.7 6.7 %attention.1 = bf16[8,8,2048]{2,1,0:T(8,128)(2,1)} custom-call(s32[4]{0:T(128)S(1)} %copy-done.16, s32[4,4]{1,0:T(4,128)S(1)} %copy-done.11, s32[4,4]{1,0:T(4,128)S(1)} %copy-done.15, bf16[4,2,8,2560]{3,2,1,0:T(8,128)(2,1)S(1)} %all-to-all-done.arrived, bf16[256,256]{1,0:T(8,128)(2,1)S(1)} %copy-done.5, bf16[256,256]{1,0:T(8,128)(2,1)S(1)} %copy-done.6, ...), custom_call_target="tpu_custom_call" | custom-call | tf_op jit(solution)/shard_map/attention/pallas_call | solution.py:364
  (23 shorter events, 0.0 us)
Async XLA Ops:
  0.6 0.7 %copy-start.11 = (s32[4,4]{1,0:T(4,128)S(1)}, s32[4,4]{1,0:T(4,128)}, u32[]{:S(2)}) copy-start(s32[4,4]{1,0:T(4,128)} %new_blocks.5) | copy-start | bytes 196
  0.6 0.7 %copy-start.16 = (s32[4]{0:T(128)S(1)}, s32[4]{0:T(128)}, u32[]{:S(2)}) copy-start(s32[4]{0:T(128)} %spread.7) | copy-start | bytes 52
  0.7 0.7 %copy-start.18 = (s32[4]{0:T(128)S(1)}, s32[4]{0:T(128)}, u32[]{:S(2)}) copy-start(s32[4]{0:T(128)} %turn.3) | copy-start | bytes 52
  1.3 0.8 %copy-start.1 = (f32[80,128]{1,0:T(8,128)S(1)}, f32[80,128]{1,0:T(8,128)}, u32[]{:S(2)}) copy-start(f32[80,128]{1,0:T(8,128)} %constant.4.clone.cosine) | copy-start | bytes 122884
  2.1 0.8 %copy-start.3 = (f32[80,128]{1,0:T(8,128)S(1)}, f32[80,128]{1,0:T(8,128)}, u32[]{:S(2)}) copy-start(f32[80,128]{1,0:T(8,128)} %constant.5.clone.sine) | copy-start | bytes 122884
  2.9 0.8 %copy-start.7 = (bf16[64,256]{1,0:T(8,128)(2,1)S(1)}, bf16[64,256]{1,0:T(8,128)(2,1)}, u32[]{:S(2)}) copy-start(bf16[64,256]{1,0:T(8,128)(2,1)} %param.14) | copy-start | bytes 98308
  3.6 0.8 %copy-start.9 = (bf16[64,256]{1,0:T(8,128)(2,1)S(1)}, bf16[64,256]{1,0:T(8,128)(2,1)}, u32[]{:S(2)}) copy-start(bf16[64,256]{1,0:T(8,128)(2,1)} %param.15) | copy-start | bytes 98308
  4.4 0.7 %copy-start.12 = (s32[4,4]{1,0:T(4,128)S(1)}, s32[4,4]{1,0:T(4,128)}, u32[]{:S(2)}) copy-start(s32[4,4]{1,0:T(4,128)} %owner.3) | copy-start | bytes 196
  5.1 0.7 %copy-start.14 = (s32[4,4]{1,0:T(4,128)S(1)}, s32[4,4]{1,0:T(4,128)}, u32[]{:S(2)}) copy-start(s32[4,4]{1,0:T(4,128)} %prefix_len.3) | copy-start | bytes 196
  5.8 9.3 %copy-start = (bf16[64,2048]{1,0:T(8,128)(2,1)S(1)}, bf16[64,2048]{1,0:T(8,128)(2,1)}, u32[]{:S(2)}) copy-start(bf16[64,2048]{1,0:T(8,128)(2,1)} %param.13) | copy-start | bytes 786436
  7.5 7.5 %copy-start.8 = (bf16[64,256]{1,0:T(8,128)(2,1)S(1)}, bf16[64,256]{1,0:T(8,128)(2,1)}, u32[]{:S(2)}) copy-start(bf16[64,256]{1,0:T(8,128)(2,1)} %param.14) | copy-start | bytes 98308
  7.5 7.5 %copy-start.10 = (bf16[64,256]{1,0:T(8,128)(2,1)S(1)}, bf16[64,256]{1,0:T(8,128)(2,1)}, u32[]{:S(2)}) copy-start(bf16[64,256]{1,0:T(8,128)(2,1)} %param.15) | copy-start | bytes 98308
  7.5 15.4 %all-to-all-start.1 = ((bf16[16,16,256]{2,1,0:T(8,128)(2,1)}), bf16[16,16,256]{2,1,0:T(8,128)(2,1)S(1)}, u32[]{:S(2)}, u32[]{:S(2)}) async-start(bf16[16,16,256]{2,1,0:T(8,128)(2,1)} %finish_pages.1), calls=%async_computation.1 | async-start | bytes 262144 | tf_op jit(solution)/shard_map/all_to_all | solution.py:362
  22.9 3.6 %copy-start.13 = (s32[4,4]{1,0:T(4,128)S(1)}, s32[4,4]{1,0:T(4,128)}, u32[]{:S(2)}) copy-start(s32[4,4]{1,0:T(4,128)} %owner.3) | copy-start | bytes 196
  23.0 3.6 %copy-start.17 = (s32[4,4]{1,0:T(4,128)S(1)}, s32[4,4]{1,0:T(4,128)}, u32[]{:S(2)}) copy-start(s32[4,4]{1,0:T(4,128)} %page_start.1) | copy-start | bytes 196
  23.0 13.7 %copy-start.6 = (bf16[256,256]{1,0:T(8,128)(2,1)S(1)}, bf16[256,256]{1,0:T(8,128)(2,1)}, u32[]{:S(2)}) copy-start(bf16[256,256]{1,0:T(8,128)(2,1)} %prefix_values.1) | copy-start | bytes 393220
  23.0 13.7 %all-to-all-start = ((bf16[4,2,8,2560]{3,2,1,0:T(8,128)(2,1)}), bf16[4,2,8,2560]{3,2,1,0:T(8,128)(2,1)S(1)}, u32[]{:S(2)}, u32[]{:S(2)}) async-start(bf16[4,2,8,2560]{3,2,1,0:T(8,128)(2,1)} %dispatch.1), calls=%async_computation | async-start | bytes 655360 | tf_op jit(solution)/shard_map/all_to_all | solution.py:347
  26.6 10.1 %copy-start.5 = (bf16[256,256]{1,0:T(8,128)(2,1)S(1)}, bf16[256,256]{1,0:T(8,128)(2,1)}, u32[]{:S(2)}) copy-start(bf16[256,256]{1,0:T(8,128)(2,1)} %prefix_keys.1) | copy-start | bytes 393220
  27.6 9.1 %copy-start.2 = (f32[80,128]{1,0:T(8,128)S(1)}, f32[80,128]{1,0:T(8,128)}, u32[]{:S(2)}) copy-start(f32[80,128]{1,0:T(8,128)} %constant.4.clone.cosine) | copy-start | bytes 122884
  27.6 9.1 %copy-start.4 = (f32[80,128]{1,0:T(8,128)S(1)}, f32[80,128]{1,0:T(8,128)}, u32[]{:S(2)}) copy-start(f32[80,128]{1,0:T(8,128)} %constant.5.clone.sine) | copy-start | bytes 122884
  27.6 9.1 %copy-start.15 = (s32[4,4]{1,0:T(4,128)S(1)}, s32[4,4]{1,0:T(4,128)}, u32[]{:S(2)}) copy-start(s32[4,4]{1,0:T(4,128)} %prefix_len.3) | copy-start | bytes 196
